TPU v7x, 512 devices: a whole 4x4x16 slice. The times are simulated.
512 devices in a mesh: facet: 64 (over z, y), pol: 4 (over x), tm: 2 (over core).
Axes of the slice: x: 4, y: 4, z: 16, core: 2. Of those that a mesh axis runs over, the one named last changes fastest.
Arguments:
- tile_spectral_lines: bfloat16 [64, 4, 2, 64, 4096], P('facet', 'pol', None, 'tm'), may hold values from -6 to 6
- taper_leading_axis: bfloat16 [64, 2, 128, 512], P('facet', 'tm'), may hold values from -0.25 to 0.25
- taper_trailing_axis: bfloat16 [64, 2, 128, 512], P('facet', 'tm'), may hold values from -0.25 to 0.25
- depth_layer_factors: bfloat16 [64, 2, 2, 128], P('facet', 'tm'), may hold values from -4 to 4
- measured_correlations: float32 [64, 8, 2, 128], P('facet', None, 'tm', 'pol'), may hold values from -6 to 6
- visibility_groups_table: int32 [64, 2, 3, 8], P('facet', 'tm'), may hold values from 0 to 130815, as said below
- antenna_links: int32 [2, 130816], replicated, may hold values from 0 to 511, as said below
- complex_receiver_factors: float32 [256, 4, 512], replicated, may hold values from -5 to 5
Outputs:
- residual: float32 [64, 8, 2, 128], P('facet', None, 'tm', 'pol')
- gain_grad: float32 [512, 1024], P(('facet', 'pol', 'tm'))
Inputs may be any that keep to these rules, and one draw needn't show every extreme that they name: `visibility_groups_table`: for each subgrid and owner, every block has a channel below 256, a count of 1 or more, and baselines offset to offset + count - 1 below 130816; the counts of one owner sum to at most 128, and some owner reaches 128 in every draw. `antenna_links`: each baseline joins two different stations.
All inputs are finite; a program needn't handle non-finite values.
Results may differ from a plain program's by a relative error of at most 0.012.
Values may be sent and summed in bfloat16 or wider, within the bound.
No kernel may reach another device: no remote copies, remote signals or barrier semaphores. Data moves between devices by JAX's collectives and lax.ppermute only.
A program may use at most 192 MiB of HBM per device.

v0:
```python
import math
import jax
import jax.numpy as jnp
import numpy as np
from jax import lax
from jax.sharding import PartitionSpec as P

FGRID = 8
FS = 4096
MC = 64
SG = 512
NPOL = 4
NW = 2
NCH = 256
NST = 512
w_chirp = 0.37
grad_scale = 0.1
feed_first = np.array([0, 0, 1, 1])
feed_second = np.array([0, 1, 0, 1])


def laid_out(blocks, dim):
    blocks = jnp.moveaxis(blocks, 0, dim)
    lengths = blocks.shape
    return blocks.reshape(*lengths[:dim], lengths[dim] * lengths[dim + 1], *lengths[dim + 2 :])


def from_everyone(shard, axis):
    copies = jnp.broadcast_to(shard, (lax.axis_size(axis), *shard.shape))
    return lax.all_to_all(copies, axis, split_axis=0, concat_axis=0, tiled=True)


def collect(shard, axis, dim):
    return laid_out(from_everyone(shard, axis), dim)


def dft_table(length):
    indices = jnp.arange(length, dtype=jnp.int32)
    product = indices[:, None] * indices[None, :] % length
    angles = 2.0 * math.pi / length * product.astype(jnp.float32)
    factor = 1.0 / math.sqrt(length)
    return (
        (jnp.cos(angles) * factor).astype(jnp.bfloat16),
        (jnp.sin(angles) * factor).astype(jnp.bfloat16),
    )


def phase_table(left_size, right_size, length):
    left_index = jnp.arange(left_size, dtype=jnp.int32)
    right_index = jnp.arange(right_size, dtype=jnp.int32)
    product = left_index[:, None] * right_index[None, :] % length
    angles = 2.0 * math.pi / length * product.astype(jnp.float32)
    return (jnp.cos(angles), -jnp.sin(angles))


def chirp_phase(row_total, side_cells):
    across = (jnp.arange(row_total, dtype=jnp.int32) - side_cells // 2).astype(jnp.float32)
    downward = (jnp.arange(side_cells, dtype=jnp.int32) - side_cells // 2).astype(jnp.float32)
    return (
        w_chirp
        * (across[:, None] * across[:, None] + downward[None, :] * downward[None, :])
        / float(side_cells * side_cells)
    )


def make_planes(sub_real, sub_imag, phase_grid, layers):
    planes_list = []
    for plane_index in range(layers):
        angles = 2.0 * math.pi * plane_index * phase_grid
        cosine = jnp.cos(angles)
        sine_part = jnp.sin(angles)
        planes_list.append(
            jnp.stack(
                [sub_real * cosine - sub_imag * sine_part, sub_real * sine_part + sub_imag * cosine]
            ).astype(jnp.bfloat16)
        )
    return jnp.stack(planes_list)


def decode_slots(block_table, slot_index):
    channels = block_table[..., 0, :]
    offsets = block_table[..., 1, :]
    amounts = block_table[..., 2, :]
    starts = jnp.cumsum(amounts, axis=-1) - amounts
    relative = slot_index[:, None] - starts[..., None, :]
    member = ((relative >= 0) & (relative < amounts[..., None, :])).astype(jnp.int32)
    slot_live = jnp.sum(member, axis=-1)
    channel = jnp.sum(member * channels[..., None, :], axis=-1)
    antenna_couple = jnp.sum(member * (offsets[..., None, :] + relative), axis=-1)
    return (slot_live, channel, antenna_couple)


def model_terms(pred_re, pred_im, obs_re, obs_im, gain_first, gain_second, slot_live):
    first_re = gain_first[..., 2 * feed_first]
    first_im = gain_first[..., 2 * feed_first + 1]
    second_re = gain_second[..., 2 * feed_second]
    second_im = gain_second[..., 2 * feed_second + 1]
    both_re = first_re * second_re + first_im * second_im
    both_im = first_im * second_re - first_re * second_im
    model_re = both_re * pred_re - both_im * pred_im
    model_im = both_re * pred_im + both_im * pred_re
    alive_mask = slot_live.astype(jnp.float32)[..., None]
    resid_re = alive_mask * (obs_re - model_re)
    resid_im = alive_mask * (obs_im - model_im)
    cross_re = second_re * pred_re + second_im * pred_im
    cross_im = second_im * pred_re - second_re * pred_im
    lead_re = -(resid_re * cross_re - resid_im * cross_im)
    lead_im = -(resid_re * cross_im + resid_im * cross_re)
    along_re = first_re * pred_re - first_im * pred_im
    along_im = first_re * pred_im + first_im * pred_re
    trail_re = -(resid_re * along_re + resid_im * along_im)
    trail_im = -(resid_re * along_im - resid_im * along_re)
    leading = jnp.stack(
        [
            lead_re[..., 0] + lead_re[..., 1],
            lead_im[..., 0] + lead_im[..., 1],
            lead_re[..., 2] + lead_re[..., 3],
            lead_im[..., 2] + lead_im[..., 3],
        ],
        axis=-1,
    )
    trailing = jnp.stack(
        [
            trail_re[..., 0] + trail_re[..., 2],
            trail_im[..., 0] + trail_im[..., 2],
            trail_re[..., 1] + trail_re[..., 3],
            trail_im[..., 1] + trail_im[..., 3],
        ],
        axis=-1,
    )
    return (resid_re, resid_im, leading, trailing)


def degrid_block(layers, rows_u, rows_v, weights_w):
    spread_v = jnp.einsum("wcuv,nv->wcun", layers, rows_v, preferred_element_type=jnp.float32)
    along_u = jnp.sum(spread_v * jnp.transpose(rows_u).astype(jnp.float32)[None, None], axis=2)
    return jnp.sum(along_u * weights_w.astype(jnp.float32)[:, None, :], axis=0)


def on_device(
    tile_spectral_lines,
    taper_leading_axis,
    taper_trailing_axis,
    depth_layer_factors,
    measured_correlations,
    visibility_groups_table,
    antenna_links,
    complex_receiver_factors,
):
    careful = lax.Precision.HIGH
    facet_total = tile_spectral_lines.shape[0]
    row_share = tile_spectral_lines.shape[3]
    spread = FS // MC
    subgrids = lax.axis_size("facet")
    source = (
        tile_spectral_lines[:, 0].astype(jnp.float32).reshape(facet_total, 2, row_share, MC, spread)
    )
    source_re = source[:, 0]
    source_im = source[:, 1]
    inner_re, inner_im = phase_table(MC, MC, MC)
    section_re = jnp.einsum("fmar,ak->fmkr", source_re, inner_re, precision=careful) - jnp.einsum(
        "fmar,ak->fmkr", source_im, inner_im, precision=careful
    )
    section_im = jnp.einsum("fmar,ak->fmkr", source_re, inner_im, precision=careful) + jnp.einsum(
        "fmar,ak->fmkr", source_im, inner_re, precision=careful
    )
    twist_re, twist_im = phase_table(MC, spread, FS)
    turned_re = section_re * twist_re - section_im * twist_im
    turned_im = section_re * twist_im + section_im * twist_re
    outer_re, outer_im = phase_table(spread, subgrids, spread)
    factor = 1.0 / math.sqrt(FS)
    contrib_re = (
        jnp.einsum("fmkr,rs->sfmk", turned_re, outer_re, precision=careful)
        - jnp.einsum("fmkr,rs->sfmk", turned_im, outer_im, precision=careful)
    ) * factor
    contrib_im = (
        jnp.einsum("fmkr,rs->sfmk", turned_re, outer_im, precision=careful)
        + jnp.einsum("fmkr,rs->sfmk", turned_im, outer_re, precision=careful)
    ) * factor
    contrib = jnp.concatenate([contrib_re, contrib_im], axis=-1).astype(jnp.bfloat16)
    table_re, table_im = dft_table(SG)
    upper_half = jnp.concatenate([table_re, table_im], axis=1).reshape(FGRID, MC, 2 * SG)
    lower_half = jnp.concatenate([-table_im, table_re], axis=1).reshape(FGRID, MC, 2 * SG)
    stacked_table = jnp.stack([upper_half, lower_half], axis=1).reshape(FGRID, 2 * MC, 2 * SG)
    received = lax.all_to_all(contrib, "facet", split_axis=0, concat_axis=1, tiled=True)
    pieces = received.reshape(FGRID, FGRID, received.shape[2], 2 * MC)
    product = jnp.einsum("ijmc,jcv->imv", pieces, stacked_table, preferred_element_type=jnp.float32)
    half_rows = product.astype(jnp.bfloat16)
    whole_rows = collect(half_rows, "tm", 1).reshape(SG, 2 * SG)
    owners = lax.axis_size("tm")
    owner_index = lax.axis_index("tm")
    row_count = SG // owners
    slots_own = taper_leading_axis.shape[2]
    flat_u = taper_leading_axis.reshape(slots_own, SG)
    flat_v = taper_trailing_axis.reshape(slots_own, SG)
    flat_w = depth_layer_factors.reshape(NW, slots_own)
    first_row = owner_index * row_count
    part_re = lax.dynamic_slice_in_dim(table_re, first_row, row_count, 0)
    part_im = lax.dynamic_slice_in_dim(table_im, first_row, row_count, 0)
    upper_rows = jnp.dot(part_re, whole_rows, preferred_element_type=jnp.float32)
    lower_rows = jnp.dot(part_im, whole_rows, preferred_element_type=jnp.float32)
    sub_real = upper_rows[:, :SG] - lower_rows[:, SG:]
    sub_imag = upper_rows[:, SG:] + lower_rows[:, :SG]
    own_part = jnp.stack([sub_real, sub_imag]).astype(jnp.bfloat16)
    subgrid = collect(own_part, "tm", 1)
    layers = make_planes(subgrid[0], subgrid[1], chirp_phase(SG, SG), NW)
    predicted = degrid_block(layers, flat_u, flat_v, flat_w)
    regrouped = lax.all_to_all(predicted[None], "pol", split_axis=2, concat_axis=0, tiled=True)
    quarter = regrouped.shape[2]
    slot_index = lax.axis_index("pol") * quarter + jnp.arange(quarter, dtype=jnp.int32)
    slot_live, channel, antenna_couple = decode_slots(
        visibility_groups_table.reshape(3, visibility_groups_table.shape[3]), slot_index
    )
    antenna_left = jnp.take(antenna_links[0], antenna_couple)
    antenna_right = jnp.take(antenna_links[1], antenna_couple)
    gains_turned = jnp.transpose(complex_receiver_factors, (0, 2, 1))
    gain_first = gains_turned[channel, antenna_left]
    gain_second = gains_turned[channel, antenna_right]
    pred_re = jnp.transpose(regrouped[:, 0])
    pred_im = jnp.transpose(regrouped[:, 1])
    observed_local = measured_correlations.reshape(NPOL, 2, quarter)
    obs_re = jnp.transpose(observed_local[:, 0])
    obs_im = jnp.transpose(observed_local[:, 1])
    resid_re, resid_im, leading, trailing = model_terms(
        pred_re, pred_im, obs_re, obs_im, gain_first, gain_second, slot_live
    )
    residual = jnp.stack([jnp.transpose(resid_re), jnp.transpose(resid_im)], axis=1).reshape(
        1, 2 * NPOL, 1, quarter
    )
    channel_ids = jnp.arange(NCH, dtype=jnp.int32)
    own_count = NST // lax.axis_size(("facet", "pol", "tm"))
    own_stations = (
        lax.axis_index(("facet", "pol", "tm")) * own_count + jnp.arange(own_count, dtype=jnp.int32)
    ).astype(jnp.float32)
    channel_float = channel_ids.astype(jnp.float32)
    ident_rows = jnp.stack([antenna_left, antenna_right, channel]).astype(jnp.float32)
    records = jnp.concatenate([ident_rows, jnp.transpose(leading), jnp.transpose(trailing)], axis=0)
    piece = lax.all_gather(records, ("facet", "pol", "tm"), axis=1, tiled=True)
    piece_rows = piece.shape[1]
    group = math.gcd(piece_rows, 8 * quarter)
    grouped = jnp.transpose(piece.reshape(11, piece_rows // group, group), (1, 0, 2))

    def one_group(carry, record_block):
        match_first = (record_block[0][:, None] == own_stations[None, :]).astype(jnp.float32)
        match_second = (record_block[1][:, None] == own_stations[None, :]).astype(jnp.float32)
        weighted = (
            match_first[:, :, None] * jnp.transpose(record_block[3:7])[:, None, :]
            + match_second[:, :, None] * jnp.transpose(record_block[7:11])[:, None, :]
        )
        onehot = (record_block[2][:, None] == channel_float[None, :]).astype(jnp.float32)
        added = jnp.dot(
            jnp.transpose(weighted.reshape(group, own_count * 4)), onehot, precision=careful
        )
        return (carry + added.reshape(own_count, 4, NCH), None)

    result, unused = lax.scan(one_group, jnp.zeros((own_count, 4, NCH), jnp.float32), grouped)
    gain_grad = grad_scale * jnp.transpose(result, (0, 2, 1)).reshape(own_count, 4 * NCH)
    return (residual, gain_grad)


def solution(mesh):
    return jax.shard_map(
        on_device,
        mesh=mesh,
        in_specs=(
            P("facet", "pol", None, "tm", None),
            P("facet", "tm", None, None),
            P("facet", "tm", None, None),
            P("facet", "tm", None, None),
            P("facet", None, "tm", "pol"),
            P("facet", "tm", None, None),
            P(),
            P(),
        ),
        out_specs=(P("facet", None, "tm", "pol"), P(("facet", "pol", "tm"), None)),
        check_vma=False,
    )
```

profile of v0, /device:TPU:1, one launch (start us, length us, event | category | flops | bytes accessed | tf_op | source)
XLA Modules:
  0.0 288.2 jit_solution(2135503734819156724)
XLA Ops:
  0.6 2.1 reshape.857
  5.4 1.7 fusion.60
  7.1 1.7 fusion.58
  8.8 1.7 fusion.38
  10.5 1.7 fusion.37
  12.6 1.1 copy.72
  13.7 19.7 %all-to-all-start = ((bf16[64,1,32,128]{3,2,1,0:T(8,128)(2,1)}), bf16[64,1,32,128]{3,2,1,0:T(8,128)(2,1)}, u32[]{:S(2)}, u32[]{:S(2)}) async-start(bf16[64,1,32,128]{3,2,1,0:T(8,128)(2,1)} %copy.72), calls=%async_computation | async-start | bytes 1048576 | tf_op jit(solution)/shard_map/all_to_all | solution.py:185
  34.4 4.2 %slice_reduce_fusion.1 = (s32[130816]{0:T(1024)S(1)}, s32[130816]{0:T(1024)S(1)}) fusion(s32[2,130816]{1,0:T(2,128)} %param.26), kind=kLoop, calls=%fused_computation.123 | loop fusion | bytes 2093056 | tf_op jit(solution)/shard_map/slice | solution.py:214
  38.6 0.7 gather_fusion.6
  39.3 0.7 gather_fusion.7
  41.5 29.9 %copy.65 = f32[256,4,512]{1,2,0:T(8,128)} copy(f32[256,4,512]{2,1,0:T(4,128)S(1)} %copy-done.1) | data formatting | bytes 4194304 | tf_op args[7]
  71.4 1.4 gather_fusion
  74.0 2.0 gather_fusion.2
  78.3 4.3 %fusion.83 = bf16[8,1,64,512]{3,2,1,0:T(8,128)(2,1)S(1)} fusion(s32[8,64]{1,0:T(8,128)S(1)} %multiply_add_fusion.3), kind=kLoop, calls=%fused_computation.133 | loop fusion | flops 4980736 | bytes 526336 | tf_op jit(solution)/shard_map/neg | solution.py:183
  82.6 4.9 %multiply_convert_fusion = (bf16[8,1,64,512]{3,2,1,0:T(8,128)(2,1)S(1)}, bf16[8,1,64,512]{3,2,1,0:T(8,128)(2,1)S(1)}) fusion(s32[8,64]{1,0:T(8,128)S(1)} %multiply_add_fusion.3), kind=kLoop, calls=%fused_computation.96 | loop fusion | flops 4718592 | bytes 1050624 | tf_op jit(solution)/shard_map/convert_element_type | solution.py:44
  89.3 1.8 fusion.36
  91.2 5.1 %all_to_all.37 = bf16[2,8,32,1024]{3,2,1,0:T(8,128)(2,1)S(1)} all-to-all(bf16[2,8,32,1024]{3,2,1,0:T(8,128)(2,1)S(1)} %broadcast_in_dim.32), channel_id=1, replica_groups=mesh['facet'=64,'pol'=4,'tm'=2] {'tm'}, dimensions={0} | all-to-all | bytes 2097152 | tf_op jit(solution)/shard_map/all_to_all | solution.py:30
  96.4 2.0 fusion.77
  98.4 2.0 fusion.78
  100.9 4.7 %all_to_all.38 = bf16[2,2,256,512]{3,2,1,0:T(8,128)(2,1)S(1)} all-to-all(bf16[2,2,256,512]{3,2,1,0:T(8,128)(2,1)S(1)} %broadcast_in_dim.33), channel_id=1, replica_groups=mesh['facet'=64,'pol'=4,'tm'=2] {'tm'}, dimensions={0} | all-to-all | bytes 2097152 | tf_op jit(solution)/shard_map/all_to_all | solution.py:30
  105.6 8.5 %fusion.74 = (bf16[1,1,512,512]{3,2,1,0:T(8,128)(2,1)S(1)}, bf16[1,1,512,512]{3,2,1,0:T(8,128)(2,1)S(1)}, bf16[1,1,512,512]{3,2,1,0:T(8,128)(2,1)S(1)}, bf16[1,1,512,512]{3,2,1,0:T(8,128)(2,1)S(1)}) fusion(bf16[1,512,512]{2,1,0:T(8,128)(2,1)S(1)} %bitcast.376, f32[512]{0:T(512)S(1)} %convert_multiply_fusion.8, bf16[1,512,512]{2,1,0:T(8,128)(2,1)S(1)} %bitcast.375), kind=kLoop, calls=%fused_computation.121 | loop fusion | flops 5505024 | bytes 3147776 | tf_op jit(solution)/shard_map/stack | solution.py:73
  114.1 0.7 fusion.39
  114.9 0.7 copy.75
  115.6 5.1 %all-to-all-start.3 = ((f32[1,2,128]{1,0,2:T(1,128)}), f32[1,2,128]{1,0,2:T(1,128)S(1)}, u32[]{:S(2)}, u32[]{:S(2)}) async-start(f32[1,2,128]{1,0,2:T(1,128)} %copy.75), calls=%async_computation.3 | async-start | bytes 131072 | tf_op jit(solution)/shard_map/all_to_all | solution.py:208
  120.8 0.7 gather_fusion.3
  122.2 3.0 %all-to-all-done.3 = f32[1,2,128]{1,0,2:T(1,128)S(1)} async-done(((f32[1,2,128]{1,0,2:T(1,128)}), f32[1,2,128]{1,0,2:T(1,128)S(1)}, u32[]{:S(2)}, u32[]{:S(2)}) %all-to-all-start.3) | async-done | bytes 1056 | tf_op jit(solution)/shard_map/all_to_all | solution.py:208
  125.4 136.5 %all-gather = f32[512,32,11]{1,2,0:T(8,128)S(1)} all-gather(f32[1,32,11]{1,2,0:T(8,128)S(1)} %maximum_bitcast_fusion), channel_id=1, replica_groups=mesh['facet'=64,'pol'=4,'tm'=2] {'facet','pol','tm'}, dimensions={0}, use_global_device_ids=true | all-gather | bytes 722304 | tf_op jit(solution)/shard_map/all_gather | solution.py:238
  262.0 0.9 copy.79
  262.9 2.3 reshape.946
  265.2 1.5 copy.93
  266.8 19.9 %while.11 = (s32[]{:T(128)}, f32[1,4,256]{2,1,0:T(4,128)S(1)}, f32[64,11,256]{2,0,1:T(8,128)S(1)}, f32[1]{0:T(128)}, s32[]{:T(128)}, /*index=5*/s32[]{:T(128)}, s32[]{}, s32[]{}, s32[]{}, s32[]{}) while((s32[]{:T(128)}, f32[1,4,256]{2,1,0:T(4,128)S(1)}, f32[64,11,256]{2,0,1:T(8,128)S(1)}, f32[1]{0:T(128)}, s32[]{:T(128)}, ...), condition=%wide.region_7.9_spmd.clone, body=%wide.region_6.8_spmd.clone.sunk | while | flops 1644807 | bytes 44223 | solution.py:256
  286.9 0.7 mul.845
  (411 shorter events, 30.8 us)
Async XLA Ops:
  0.6 113.5 %copy-start = (bf16[1,1,128,512]{3,2,1,0:T(8,128)(2,1)S(1)}, bf16[1,1,128,512]{3,2,1,0:T(8,128)(2,1)}, u32[]{:S(2)}) copy-start(bf16[1,1,128,512]{3,2,1,0:T(8,128)(2,1)} %param.22) | copy-start | bytes 393220
  12.3 21.2 %copy-start.2 = (bf16[1,1,128,512]{3,2,1,0:T(8,128)(2,1)S(1)}, bf16[1,1,128,512]{3,2,1,0:T(8,128)(2,1)}, u32[]{:S(2)}) copy-start(bf16[1,1,128,512]{3,2,1,0:T(8,128)(2,1)} %param.21) | copy-start | bytes 393220
  12.3 21.2 %copy-start.8 = (s32[1,1,3,8]{3,1,2,0:T(1,128)S(1)}, s32[1,1,3,8]{3,1,2,0:T(1,128)}, u32[]{:S(2)}) copy-start(s32[1,1,3,8]{3,1,2,0:T(1,128)} %param.25) | copy-start | bytes 292
  13.7 75.6 %all-to-all-start = ((bf16[64,1,32,128]{3,2,1,0:T(8,128)(2,1)}), bf16[64,1,32,128]{3,2,1,0:T(8,128)(2,1)}, u32[]{:S(2)}, u32[]{:S(2)}) async-start(bf16[64,1,32,128]{3,2,1,0:T(8,128)(2,1)} %copy.72), calls=%async_computation | async-start | bytes 1048576 | tf_op jit(solution)/shard_map/all_to_all | solution.py:185
  33.5 8.0 %copy-start.1 = (f32[256,4,512]{2,1,0:T(4,128)S(1)}, f32[256,4,512]{2,1,0:T(4,128)}, u32[]{:S(2)}) copy-start(f32[256,4,512]{2,1,0:T(4,128)} %param.27) | copy-start | bytes 6291460
  41.5 35.1 %copy-start.11 = (s32[4]{0:T(128)S(1)}, s32[4]{0:T(128)}, u32[]{:S(2)}) copy-start(s32[4]{0:T(128)} %constant.187) | copy-start | bytes 52
  41.5 35.7 %copy-start.10 = (s32[4]{0:T(128)S(1)}, s32[4]{0:T(128)}, u32[]{:S(2)}) copy-start(s32[4]{0:T(128)} %constant.189) | copy-start | bytes 52
  87.5 0.7 copy-start.13
  87.5 1.2 copy-start.6
  114.1 0.8 copy-start.9
  114.1 6.6 %copy-start.3 = (f32[32,4]{1,0:T(8,128)S(1)}, f32[32,4]{1,0:T(8,128)}, u32[]{:S(2)}) copy-start(f32[32,4]{1,0:T(8,128)} %gather_fusion.2) | copy-start | bytes 1540
  114.1 8.1 %copy-start.12 = (s32[32]{0:T(128)S(1)}, s32[32]{0:T(128)}, u32[]{:S(2)}) copy-start(s32[32]{0:T(128)} %get-tuple-element.68) | copy-start | bytes 388
  114.1 11.2 %copy-start.4 = (f32[4,1,32]{2,1,0:T(1,128)S(1)}, f32[4,1,32]{2,1,0:T(1,128)}, u32[]{:S(2)}) copy-start(f32[4,1,32]{2,1,0:T(1,128)} %get-tuple-element.107) | copy-start | bytes 1540
  114.1 11.3 %copy-start.5 = (f32[3,32]{1,0:T(4,128)S(1)}, f32[3,32]{1,0:T(4,128)}, u32[]{:S(2)}) copy-start(f32[3,32]{1,0:T(4,128)} %add_convert_fusion) | copy-start | bytes 1156
  115.6 9.6 %all-to-all-start.3 = ((f32[1,2,128]{1,0,2:T(1,128)}), f32[1,2,128]{1,0,2:T(1,128)S(1)}, u32[]{:S(2)}, u32[]{:S(2)}) async-start(f32[1,2,128]{1,0,2:T(1,128)} %copy.75), calls=%async_computation.3 | async-start | bytes 131072 | tf_op jit(solution)/shard_map/all_to_all | solution.py:208
  265.2 1.6 copy-start.7
where the time goes:
time: 289 us; the launch traced here: 288 us
  blocking collectives  146 us (51%)
  local copies, waits for them, and re-layouts  55.5 us (19%)
  matrix products  30.4 us (11%)
  other arithmetic  24.8 us (9%)
  starting transfers between devices  24.8 us (9%)
  waiting for transfers between devices  3 us (1%)
    all_gather x1, blocking collectives, on_device(): piece = lax.all_gather(records, ('facet', 'pol', 'tm'), axis=1, tiled=True)  137 us
    unnamed x31, local copies, waits for them, and re-layouts  34.2 us
    all_to_all x1, starting transfers between devices, on_device(): lax.all_to_all(contrib, 'facet', split_axis=0, concat_axis=1, tiled=True)  19.7 us
    dot_general x64, matrix products, one_group(): jnp.dot(jnp.transpose(weighted.reshape(group, own_count * 4)), onehot, pr...  14.9 us
    all_to_all x2, blocking collectives, from_everyone(): return lax.all_to_all(copies, axis, split_axis=0, concat_axis=0, tiled=True)  9.81 us
    another operation x1, other arithmetic, make_planes(): jnp.stack([sub_real * cosine - sub_imag * sine_part, sub_real * sine_part...  8.45 us
  transfers between devices with their start and end apart: 2, of which 1 were waited for; matrix products, arithmetic and copies ran while one was open for 20% of the time, Pallas kernels for 0%

commit v1 on v0

--- a/solution.py
+++ b/solution.py
@@ -17,6 +17,17 @@
 grad_scale = 0.1
 feed_first = np.array([0, 0, 1, 1])
 feed_second = np.array([0, 1, 0, 1])
+
+
+def cut_along(x, dim, peers):
+    before, after = (x.shape[:dim], x.shape[dim + 1 :])
+    return jnp.moveaxis(x.reshape(*before, peers, -1, *after), dim, 0)
+
+
+def joined_along(blocks, dim):
+    shape = list(blocks.shape[1:])
+    shape[dim] *= blocks.shape[0]
+    return jnp.moveaxis(blocks, 0, dim).reshape(shape)
 
 
 def laid_out(blocks, dim):
@@ -205,7 +216,14 @@
     subgrid = collect(own_part, "tm", 1)
     layers = make_planes(subgrid[0], subgrid[1], chirp_phase(SG, SG), NW)
     predicted = degrid_block(layers, flat_u, flat_v, flat_w)
-    regrouped = lax.all_to_all(predicted[None], "pol", split_axis=2, concat_axis=0, tiled=True)
+    size, mine = (lax.axis_size("pol"), lax.axis_index("pol"))
+    tiles = cut_along(predicted[None], 2, size)
+    outs = [tiles[mine]]
+    for step in range(1, size):
+        sent = tiles[(mine + step) % size]
+        outs.append(lax.ppermute(sent, "pol", [(i, (i + step) % size) for i in range(size)]))
+    tiles = jnp.stack(outs)[(mine - jnp.arange(size)) % size]
+    regrouped = joined_along(tiles, 0)
     quarter = regrouped.shape[2]
     slot_index = lax.axis_index("pol") * quarter + jnp.arange(quarter, dtype=jnp.int32)
     slot_live, channel, antenna_couple = decode_slots(

time: 289 us -> 296 us (1.024)
  starting transfers between devices: 24.8 us -> 31.2 us
    ppermute x0 -> x3, starting transfers between devices: none -> 11.5 us  [on_device(): lax.ppermute(sent, 'pol', [(i, (i + step) % size) for i in range(size)])]
    all_to_all x1 -> x0, starting transfers between devices: 5.1 us -> none  [on_device(): lax.all_to_all(predicted[None], 'pol', split_axis=2, concat_axis=0, tiled...]
    all_to_all x1 -> x0, waiting for transfers between devices: 3 us -> none  [on_device(): lax.all_to_all(predicted[None], 'pol', split_axis=2, concat_axis=0, tiled...]
    unnamed x31 -> x33, local copies, waits for them, and re-layouts: 34.2 us -> 34.1 us
  transfers between devices with their start and end apart: 2 -> 4, of which waited for: 1 -> 1; matrix products, arithmetic and copies ran while one was open for 20% -> 20% of each run, Pallas kernels for 0% -> 0%
where the time goes in v1:
time: 296 us
  blocking collectives  148 us (50%)
  local copies, waits for them, and re-layouts  54.6 us (18%)
  starting transfers between devices  31.2 us (11%)
  matrix products  30.4 us (10%)
  other arithmetic  27.3 us (9%)
    all_gather x1, blocking collectives, on_device(): piece = lax.all_gather(records, ('facet', 'pol', 'tm'), axis=1, tiled=True)  138 us
    unnamed x33, local copies, waits for them, and re-layouts  34.1 us
    all_to_all x1, starting transfers between devices, on_device(): lax.all_to_all(contrib, 'facet', split_axis=0, concat_axis=1, tiled=True)  19.7 us
    dot_general x64, matrix products, one_group(): jnp.dot(jnp.transpose(weighted.reshape(group, own_count * 4)), onehot, pr...  14.9 us
    ppermute x3, starting transfers between devices, on_device(): lax.ppermute(sent, 'pol', [(i, (i + step) % size) for i in range(size)])  11.5 us
    all_to_all x2, blocking collectives, from_everyone(): return lax.all_to_all(copies, axis, split_axis=0, concat_axis=0, tiled=True)  9.89 us
    another operation x1, other arithmetic, make_planes(): jnp.stack([sub_real * cosine - sub_imag * sine_part, sub_real * sine_part...  8.45 us
  transfers between devices with their start and end apart: 4, of which 1 were waited for; matrix products, arithmetic and copies ran while one was open for 20% of the time, Pallas kernels for 0%

profile of v1, /device:TPU:1, one launch (start us, length us, event | category | flops | bytes accessed | tf_op | source)
XLA Modules:
  0.0 295.7 jit_solution(11809676976456121613)
XLA Ops:
  0.6 2.1 reshape.916
  5.4 1.7 fusion.60
  7.1 1.7 fusion.58
  8.8 1.7 fusion.38
  10.5 1.7 fusion.37
  12.6 1.2 copy.71
  13.7 19.7 %all-to-all-start = ((bf16[64,1,32,128]{3,2,1,0:T(8,128)(2,1)}), bf16[64,1,32,128]{3,2,1,0:T(8,128)(2,1)}, u32[]{:S(2)}, u32[]{:S(2)}) async-start(bf16[64,1,32,128]{3,2,1,0:T(8,128)(2,1)} %copy.71), calls=%async_computation | async-start | bytes 1048576 | tf_op jit(solution)/shard_map/all_to_all | solution.py:196
  34.4 4.2 %slice_reduce_fusion.1 = (s32[130816]{0:T(1024)S(1)}, s32[130816]{0:T(1024)S(1)}) fusion(s32[2,130816]{1,0:T(2,128)} %param.26), kind=kLoop, calls=%fused_computation.124 | loop fusion | bytes 2093056 | tf_op jit(solution)/shard_map/slice | solution.py:232
  38.6 0.7 gather_fusion.7
  42.8 29.9 %copy.64 = f32[256,4,512]{1,2,0:T(8,128)} copy(f32[256,4,512]{2,1,0:T(4,128)S(1)} %copy-done.1) | data formatting | bytes 4194304 | tf_op args[7]
  72.7 1.3 gather_fusion
  75.2 1.3 gather_fusion.2
  78.9 1.3 add_convert_fusion
  81.3 4.3 %fusion.83 = bf16[8,1,64,512]{3,2,1,0:T(8,128)(2,1)S(1)} fusion(s32[8,64]{1,0:T(8,128)S(1)} %multiply_add_fusion.3), kind=kLoop, calls=%fused_computation.134 | loop fusion | flops 4980736 | bytes 526336 | tf_op jit(solution)/shard_map/neg | solution.py:194
  85.6 4.9 %multiply_convert_fusion = (bf16[8,1,64,512]{3,2,1,0:T(8,128)(2,1)S(1)}, bf16[8,1,64,512]{3,2,1,0:T(8,128)(2,1)S(1)}) fusion(s32[8,64]{1,0:T(8,128)S(1)} %multiply_add_fusion.3), kind=kLoop, calls=%fused_computation.97 | loop fusion | flops 4718592 | bytes 1050624 | tf_op jit(solution)/shard_map/convert_element_type | solution.py:55
  92.3 1.7 fusion.36
  94.2 5.2 %all_to_all.19 = bf16[2,8,32,1024]{3,2,1,0:T(8,128)(2,1)S(1)} all-to-all(bf16[2,8,32,1024]{3,2,1,0:T(8,128)(2,1)S(1)} %broadcast_in_dim.30), channel_id=1, replica_groups=mesh['facet'=64,'pol'=4,'tm'=2] {'tm'}, dimensions={0} | all-to-all | bytes 2097152 | tf_op jit(solution)/shard_map/all_to_all | solution.py:41
  99.5 2.0 fusion.77
  101.5 2.0 fusion.78
  104.0 4.7 %all_to_all.20 = bf16[2,2,256,512]{3,2,1,0:T(8,128)(2,1)S(1)} all-to-all(bf16[2,2,256,512]{3,2,1,0:T(8,128)(2,1)S(1)} %broadcast_in_dim.31), channel_id=1, replica_groups=mesh['facet'=64,'pol'=4,'tm'=2] {'tm'}, dimensions={0} | all-to-all | bytes 2097152 | tf_op jit(solution)/shard_map/all_to_all | solution.py:41
  108.7 8.4 %fusion.74 = (bf16[1,1,512,512]{3,2,1,0:T(8,128)(2,1)S(1)}, bf16[1,1,512,512]{3,2,1,0:T(8,128)(2,1)S(1)}, bf16[1,1,512,512]{3,2,1,0:T(8,128)(2,1)S(1)}, bf16[1,1,512,512]{3,2,1,0:T(8,128)(2,1)S(1)}) fusion(bf16[1,512,512]{2,1,0:T(8,128)(2,1)S(1)} %bitcast.338, f32[512]{0:T(512)S(1)} %copy-done.3, bf16[1,512,512]{2,1,0:T(8,128)(2,1)S(1)} %bitcast.337), kind=kLoop, calls=%fused_computation.122 | loop fusion | flops 5505024 | bytes 3147776 | tf_op jit(solution)/shard_map/stack | solution.py:84
  117.2 0.7 fusion.39
  118.1 3.1 %collective-permute-start = (f32[1,2,32]{2,1,0:T(2,128)S(1)}, f32[1,2,32]{2,1,0:T(2,128)S(1)}, u32[]{:S(2)}, u32[]{:S(2)}) collective-permute-start(f32[1,2,32]{2,1,0:T(2,128)S(1)} %bitcast.358), channel_id=1, source_target_pairs={{0,2},{2,4},{4,6},{6,0},{1,3},{3,5},{5,7},{7,1},{8,10},{10,12},{12... | collective-permute-start | bytes 776 | tf_op jit(solution)/shard_map/ppermute | solution.py:224
  121.2 5.3 %collective-permute-start.1 = (f32[1,2,32]{2,1,0:T(2,128)S(1)}, f32[1,2,32]{2,1,0:T(2,128)S(1)}, u32[]{:S(2)}, u32[]{:S(2)}) collective-permute-start(f32[1,2,32]{2,1,0:T(2,128)S(1)} %bitcast.357), channel_id=1, source_target_pairs={{0,4},{2,6},{4,0},{6,2},{1,5},{3,7},{5,1},{7,3},{8,12},{10,14},{12... | collective-permute-start | bytes 776 | tf_op jit(solution)/shard_map/ppermute | solution.py:224
  126.5 3.1 %collective-permute-start.2 = (f32[1,2,32]{2,1,0:T(2,128)S(1)}, f32[1,2,32]{2,1,0:T(2,128)S(1)}, u32[]{:S(2)}, u32[]{:S(2)}) collective-permute-start(f32[1,2,32]{2,1,0:T(2,128)S(1)} %bitcast.356), channel_id=1, source_target_pairs={{0,6},{2,0},{4,2},{6,4},{1,7},{3,1},{5,3},{7,5},{8,14},{10,8},{12,... | collective-permute-start | bytes 776 | tf_op jit(solution)/shard_map/ppermute | solution.py:224
  129.6 1.2 collective-permute-done.2
  131.7 137.7 %all-gather = f32[512,32,11]{1,2,0:T(8,128)S(1)} all-gather(f32[1,32,11]{1,2,0:T(8,128)S(1)} %maximum_bitcast_fusion), channel_id=1, replica_groups=mesh['facet'=64,'pol'=4,'tm'=2] {'facet','pol','tm'}, dimensions={0}, use_global_device_ids=true | all-gather | bytes 722304 | tf_op jit(solution)/shard_map/all_gather | solution.py:256
  269.4 0.9 copy.76
  270.3 2.3 reshape.1017
  272.6 1.6 copy.90
  274.2 19.9 %while.11 = (s32[]{:T(128)}, f32[1,4,256]{2,1,0:T(4,128)S(1)}, f32[64,11,256]{2,0,1:T(8,128)S(1)}, f32[1]{0:T(128)}, s32[]{:T(128)}, /*index=5*/s32[]{:T(128)}, s32[]{}, s32[]{}, s32[]{}, s32[]{}) while((s32[]{:T(128)}, f32[1,4,256]{2,1,0:T(4,128)S(1)}, f32[64,11,256]{2,0,1:T(8,128)S(1)}, f32[1]{0:T(128)}, s32[]{:T(128)}, ...), condition=%wide.region_7.9_spmd.clone, body=%wide.region_6.8_spmd.clone.sunk | while | flops 1644807 | bytes 44223 | solution.py:274
  294.3 0.7 mul.845
  (422 shorter events, 33.8 us)
Async XLA Ops:
  0.6 116.6 %copy-start = (bf16[1,1,128,512]{3,2,1,0:T(8,128)(2,1)S(1)}, bf16[1,1,128,512]{3,2,1,0:T(8,128)(2,1)}, u32[]{:S(2)}) copy-start(bf16[1,1,128,512]{3,2,1,0:T(8,128)(2,1)} %param.22) | copy-start | bytes 393220
  12.3 21.2 %copy-start.2 = (bf16[1,1,128,512]{3,2,1,0:T(8,128)(2,1)S(1)}, bf16[1,1,128,512]{3,2,1,0:T(8,128)(2,1)}, u32[]{:S(2)}) copy-start(bf16[1,1,128,512]{3,2,1,0:T(8,128)(2,1)} %param.21) | copy-start | bytes 393220
  12.3 21.3 %copy-start.11 = (s32[1,1,3,8]{3,1,2,0:T(1,128)S(1)}, s32[1,1,3,8]{3,1,2,0:T(1,128)}, u32[]{:S(2)}) copy-start(s32[1,1,3,8]{3,1,2,0:T(1,128)} %param.25) | copy-start | bytes 292
  13.7 78.6 %all-to-all-start = ((bf16[64,1,32,128]{3,2,1,0:T(8,128)(2,1)}), bf16[64,1,32,128]{3,2,1,0:T(8,128)(2,1)}, u32[]{:S(2)}, u32[]{:S(2)}) async-start(bf16[64,1,32,128]{3,2,1,0:T(8,128)(2,1)} %copy.71), calls=%async_computation | async-start | bytes 1048576 | tf_op jit(solution)/shard_map/all_to_all | solution.py:196
  33.5 9.3 %copy-start.1 = (f32[256,4,512]{2,1,0:T(4,128)S(1)}, f32[256,4,512]{2,1,0:T(4,128)}, u32[]{:S(2)}) copy-start(f32[256,4,512]{2,1,0:T(4,128)} %param.27) | copy-start | bytes 6291460
  34.3 38.3 %copy-start.7 = (s32[32]{0:T(128)}, s32[32]{0:T(128)S(1)}, u32[]{:S(2)}) copy-start(s32[32]{0:T(128)S(1)} %get-tuple-element.69) | copy-start | bytes 388
  42.8 35.0 %copy-start.13 = (s32[32]{0:T(128)S(1)}, s32[32]{0:T(128)}, u32[]{:S(2)}) copy-start(s32[32]{0:T(128)} %get-tuple-element.68) | copy-start | bytes 388
  90.5 0.7 copy-start.14
  90.5 1.2 copy-start.8
  104.0 4.8 %copy-start.3 = (f32[512]{0:T(512)S(1)}, f32[512]{0:T(512)}, u32[]{:S(2)}) copy-start(f32[512]{0:T(512)} %convert_multiply_fusion.8) | copy-start | bytes 6148
  117.2 0.8 copy-start.12
  117.2 14.3 %copy-start.4 = (f32[4,1,32]{2,1,0:T(1,128)S(1)}, f32[4,1,32]{2,1,0:T(1,128)}, u32[]{:S(2)}) copy-start(f32[4,1,32]{2,1,0:T(1,128)} %get-tuple-element.106) | copy-start | bytes 1540
  117.2 14.3 %copy-start.5 = (f32[4,1,32]{2,1,0:T(1,128)S(1)}, f32[4,1,32]{2,1,0:T(1,128)}, u32[]{:S(2)}) copy-start(f32[4,1,32]{2,1,0:T(1,128)} %get-tuple-element.107) | copy-start | bytes 1540
  117.2 14.3 %copy-start.10 = (f32[32]{0:T(128)S(1)}, f32[32]{0:T(128)}, u32[]{:S(2)}) copy-start(f32[32]{0:T(128)} %convert_element_type.323) | copy-start | bytes 388
  117.2 14.5 %copy-start.6 = (f32[3,32]{1,0:T(4,128)S(1)}, f32[3,32]{1,0:T(4,128)}, u32[]{:S(2)}) copy-start(f32[3,32]{1,0:T(4,128)} %add_convert_fusion) | copy-start | bytes 1156
  118.1 11.5 %collective-permute-start = (f32[1,2,32]{2,1,0:T(2,128)S(1)}, f32[1,2,32]{2,1,0:T(2,128)S(1)}, u32[]{:S(2)}, u32[]{:S(2)}) collective-permute-start(f32[1,2,32]{2,1,0:T(2,128)S(1)} %bitcast.358), channel_id=1, source_target_pairs={{0,2},{2,4},{4,6},{6,0},{1,3},{3,5},{5,7},{7,1},{8,10},{10,12},{12... | collective-permute-start | bytes 776 | tf_op jit(solution)/shard_map/ppermute | solution.py:224
  121.2 8.4 %collective-permute-start.1 = (f32[1,2,32]{2,1,0:T(2,128)S(1)}, f32[1,2,32]{2,1,0:T(2,128)S(1)}, u32[]{:S(2)}, u32[]{:S(2)}) collective-permute-start(f32[1,2,32]{2,1,0:T(2,128)S(1)} %bitcast.357), channel_id=1, source_target_pairs={{0,4},{2,6},{4,0},{6,2},{1,5},{3,7},{5,1},{7,3},{8,12},{10,14},{12... | collective-permute-start | bytes 776 | tf_op jit(solution)/shard_map/ppermute | solution.py:224
  126.5 4.3 %collective-permute-start.2 = (f32[1,2,32]{2,1,0:T(2,128)S(1)}, f32[1,2,32]{2,1,0:T(2,128)S(1)}, u32[]{:S(2)}, u32[]{:S(2)}) collective-permute-start(f32[1,2,32]{2,1,0:T(2,128)S(1)} %bitcast.356), channel_id=1, source_target_pairs={{0,6},{2,0},{4,2},{6,4},{1,7},{3,1},{5,3},{7,5},{8,14},{10,8},{12,... | collective-permute-start | bytes 776 | tf_op jit(solution)/shard_map/ppermute | solution.py:224
  272.6 1.6 copy-start.9
